TPU v7x, 768 devices: a whole 4x8x12 slice. The times are simulated.
768 devices in a mesh: outer: 12 (over z_lo, core), inner: 64 (over z_hi, x, y).
Axes of the slice: x: 4, y: 8, z: 12 (z_hi: 2, z_lo: 6; z = z_hi * 6 + z_lo), core: 2. Of those that a mesh axis runs over, the one named last changes fastest.
Arguments:
- image_emb: float32 [196608, 1152], P(('outer', 'inner')), may hold values from -0.17677669 to 0.17677669
- text_emb: float32 [196608, 1152], P(('outer', 'inner')), may hold values from -0.17677669 to 0.17677669
- score_scale: float32 [1], replicated, may hold values from 4 to 16
- logit_bias: float32 [1], replicated, may hold values from -4 to -1
Outputs:
- grad_image: float32 [196608, 1152], P(('outer', 'inner'))
- grad_text: float32 [196608, 1152], P(('outer', 'inner'))
- row_loss: float32 [196608], P(('outer', 'inner'))
All inputs are finite; a program needn't handle non-finite values.
Results may differ from a plain program's by a relative error of at most 0.0042.
Values may be sent and summed in bfloat16 or wider, within the bound.
A program may use at most 32 MiB of HBM per device.

v0:
```python
import jax
import jax.numpy as jnp
from jax import lax
from jax.sharding import PartitionSpec as P

INNER_STEPS = 2
OUTER_STEPS = 2


def shifted(block, axis, distance):
    devices = range(lax.axis_size(axis))
    route = [((i - distance) % len(devices), i) for i in devices]
    return lax.ppermute(block, axis, route)


def block_meeting_step(
    picture_split_rows, caption_square, sharpness_scale, rotation_steps, matching_couples
):
    score_grid = (
        sharpness_scale
        * lax.dot_general(
            picture_split_rows,
            caption_square,
            (((1,), (1,)), ((), ())),
            preferred_element_type=jnp.float32,
        )
        + rotation_steps
    )
    if matching_couples:
        desired_signs = jnp.eye(score_grid.shape[0], dtype=jnp.float32)
    else:
        desired_signs = jnp.zeros_like(score_grid)
    loss_values = jax.nn.softplus((1.0 - 2.0 * desired_signs) * score_grid)
    coefficient_split_rows = (
        sharpness_scale * (jax.nn.sigmoid(score_grid) - desired_signs)
    ).astype(jnp.bfloat16)
    return (coefficient_split_rows, jnp.sum(loss_values, axis=1))


def per_device(image_emb, text_emb, score_scale, logit_bias):
    sharpness_scale = score_scale[0]
    rotation_steps = logit_bias[0]
    picture_split_rows = image_emb.astype(jnp.bfloat16)
    own_text = text_emb.astype(jnp.bfloat16)
    row_count = image_emb.shape[0]
    width = image_emb.shape[1]
    grad_image = jnp.zeros((row_count, width), jnp.float32)
    grad_text = jnp.zeros((row_count, width), jnp.float32)
    loss_total = jnp.zeros((row_count,), jnp.float32)
    outer_block = own_text
    for outer_step in range(OUTER_STEPS):
        if outer_step > 0:
            outer_block = shifted(outer_block, "outer", 1)
        current_position = outer_block
        carried = jnp.zeros((row_count, width), jnp.float32)
        for inner_step in range(INNER_STEPS):
            matching_couples = outer_step == 0 and inner_step == 0
            if inner_step > 0:
                current_position = shifted(current_position, "inner", 1)
            coefficient_split_rows, loss_values = block_meeting_step(
                picture_split_rows,
                current_position,
                sharpness_scale,
                rotation_steps,
                matching_couples,
            )
            grad_image = grad_image + jnp.dot(
                coefficient_split_rows, current_position, preferred_element_type=jnp.float32
            )
            loss_total = loss_total + loss_values
            partial_value = lax.dot_general(
                coefficient_split_rows,
                picture_split_rows,
                (((0,), (0,)), ((), ())),
                preferred_element_type=jnp.float32,
            )
            if inner_step > 0:
                carried = shifted(carried, "inner", 1)
            carried = carried + partial_value
        carried = shifted(carried, "inner", -(INNER_STEPS - 1))
        if outer_step > 0:
            carried = shifted(carried, "outer", -outer_step)
        grad_text = grad_text + carried
    row_loss = loss_total / (OUTER_STEPS * INNER_STEPS * row_count)
    return (grad_image, grad_text, row_loss)


def solution(mesh):
    return jax.shard_map(
        per_device,
        mesh=mesh,
        in_specs=(P(("outer", "inner"), None), P(("outer", "inner"), None), P(), P()),
        out_specs=(P(("outer", "inner"), None), P(("outer", "inner"), None), P(("outer", "inner"))),
        check_vma=False,
    )
```

profile of v0, /device:TPU:193, one launch (start us, length us, event | category | flops | bytes accessed | tf_op | source)
XLA Modules:
  0.0 321.7 jit_solution(3854105639259563420)
XLA Ops:
  0.6 0.0 copy-start
  0.6 1.4 convert_element_type.22
  2.1 5.8 %collective-permute-start.1 = (bf16[256,1152]{1,0:T(8,128)(2,1)S(1)}, bf16[256,1152]{1,0:T(8,128)(2,1)S(1)}, u32[]{:S(2)}, u32[]{:S(2)}) collective-permute-start(bf16[256,1152]{1,0:T(8,128)(2,1)S(1)} %convert_element_type.22), channel_id=1, source_target_pairs={{704,0},{0,64},{64,128},{128,192},{192,256},{256,320},{320,384},{3... | collective-permute-start | bytes 1769480 | tf_op jit(solution)/shard_map/ppermute | solution.py:13
  8.5 0.0 copy-done
  8.5 0.1 convert_element_type.21
  9.2 5.4 %collective-permute-done.1 = bf16[256,1152]{1,0:T(8,128)(2,1)S(1)} collective-permute-done((bf16[256,1152]{1,0:T(8,128)(2,1)S(1)}, bf16[256,1152]{1,0:T(8,128)(2,1)S(1)}, u32[]{:S(2)}, u32[]{:S(2)}) %collective-permute-start.1) | collective-permute-done | bytes 589856 | tf_op jit(solution)/shard_map/ppermute | solution.py:13
  14.7 0.5 fusion.6
  15.2 0.4 fusion.8
  15.5 3.2 collective-permute-start.5
  18.7 3.2 collective-permute-start.2
  22.0 0.5 fusion.4
  22.5 0.4 fusion.9
  22.8 3.2 collective-permute-start.3
  26.1 86.0 %collective-permute-done.2 = bf16[256,1152]{1,0:T(8,128)(2,1)S(1)} collective-permute-done((bf16[256,1152]{1,0:T(8,128)(2,1)S(1)}, bf16[256,1152]{1,0:T(8,128)(2,1)S(1)}, u32[]{:S(2)}, u32[]{:S(2)}) %collective-permute-start.2) | collective-permute-done | bytes 589856 | tf_op jit(solution)/shard_map/ppermute | solution.py:13
  112.0 0.5 fusion.7
  112.5 0.0 collective-permute-done.5
  112.5 0.4 convolution_add_fusion
  112.9 1.9 collective-permute-start.6
  114.8 3.4 %collective-permute-start = (bf16[256,1152]{1,0:T(8,128)(2,1)S(1)}, bf16[256,1152]{1,0:T(8,128)(2,1)S(1)}, u32[]{:S(2)}, u32[]{:S(2)}) collective-permute-start(bf16[256,1152]{1,0:T(8,128)(2,1)S(1)} %convert_element_type.22), channel_id=1, source_target_pairs={{63,0},{0,1},{1,2},{2,3},{3,4},{4,5},{5,6},{6,7},{7,8},{8,9},{9,10... | collective-permute-start | bytes 1769480 | tf_op jit(solution)/shard_map/ppermute | solution.py:13
  118.2 87.6 %collective-permute-done = bf16[256,1152]{1,0:T(8,128)(2,1)S(1)} collective-permute-done((bf16[256,1152]{1,0:T(8,128)(2,1)S(1)}, bf16[256,1152]{1,0:T(8,128)(2,1)S(1)}, u32[]{:S(2)}, u32[]{:S(2)}) %collective-permute-start) | collective-permute-done | bytes 589856 | tf_op jit(solution)/shard_map/ppermute | solution.py:13
  205.8 0.5 fusion.5
  206.3 0.0 collective-permute-done.3
  206.4 0.4 convolution_add_fusion.1
  206.7 1.9 collective-permute-start.4
  208.7 0.0 collective-permute-done.6
  208.7 8.9 %collective-permute-start.7 = (f32[256,1152]{1,0:T(8,128)S(1)}, f32[256,1152]{1,0:T(8,128)S(1)}, u32[]{:S(2)}, u32[]{:S(2)}) collective-permute-start(f32[256,1152]{1,0:T(8,128)S(1)} %collective-permute-done.6), channel_id=1, source_target_pairs={{64,0},{128,64},{192,128},{256,192},{320,256},{384,320},{448,384},... | collective-permute-start | bytes 3538952 | tf_op jit(solution)/shard_map/ppermute | solution.py:13
  217.6 0.4 fusion.10
  218.0 0.4 convolution_add_fusion.4
  218.4 0.4 convolution_add_fusion.3
  218.9 0.6 add_multiply_fusion
  219.4 1.4 convolution_add_fusion.2
  220.9 8.2 %collective-permute-done.4 = f32[256,1152]{1,0:T(8,128)S(1)} collective-permute-done((f32[256,1152]{1,0:T(8,128)S(1)}, f32[256,1152]{1,0:T(8,128)S(1)}, u32[]{:S(2)}, u32[]{:S(2)}) %collective-permute-start.4) | collective-permute-done | bytes 1179680 | tf_op jit(solution)/shard_map/ppermute | solution.py:13
  229.1 91.5 %collective-permute-done.7 = f32[256,1152]{1,0:T(8,128)S(1)} collective-permute-done((f32[256,1152]{1,0:T(8,128)S(1)}, f32[256,1152]{1,0:T(8,128)S(1)}, u32[]{:S(2)}, u32[]{:S(2)}) %collective-permute-start.7) | collective-permute-done | bytes 1179680 | tf_op jit(solution)/shard_map/ppermute | solution.py:13
  320.5 1.1 add.84
Async XLA Ops:
  0.6 7.9 %copy-start = (f32[256,1152]{1,0:T(8,128)S(1)}, f32[256,1152]{1,0:T(8,128)}, u32[]{:S(2)}) copy-start(f32[256,1152]{1,0:T(8,128)} %param.4) | copy-start | bytes 3538948
  2.1 12.6 %collective-permute-start.1 = (bf16[256,1152]{1,0:T(8,128)(2,1)S(1)}, bf16[256,1152]{1,0:T(8,128)(2,1)S(1)}, u32[]{:S(2)}, u32[]{:S(2)}) collective-permute-start(bf16[256,1152]{1,0:T(8,128)(2,1)S(1)} %convert_element_type.22), channel_id=1, source_target_pairs={{704,0},{0,64},{64,128},{128,192},{192,256},{256,320},{320,384},{3... | collective-permute-start | bytes 1769480 | tf_op jit(solution)/shard_map/ppermute | solution.py:13
  15.5 97.0 %collective-permute-start.5 = (f32[256,1152]{1,0:T(8,128)S(1)}, f32[256,1152]{1,0:T(8,128)S(1)}, u32[]{:S(2)}, u32[]{:S(2)}) collective-permute-start(f32[256,1152]{1,0:T(8,128)S(1)} %fusion.8), channel_id=1, source_target_pairs={{63,0},{0,1},{1,2},{2,3},{3,4},{4,5},{5,6},{6,7},{7,8},{8,9},{9,10... | collective-permute-start | bytes 3538952 | tf_op jit(solution)/shard_map/ppermute | solution.py:13
  18.7 93.3 %collective-permute-start.2 = (bf16[256,1152]{1,0:T(8,128)(2,1)S(1)}, bf16[256,1152]{1,0:T(8,128)(2,1)S(1)}, u32[]{:S(2)}, u32[]{:S(2)}) collective-permute-start(bf16[256,1152]{1,0:T(8,128)(2,1)S(1)} %collective-permute-done.1), channel_id=1, source_target_pairs={{63,0},{0,1},{1,2},{2,3},{3,4},{4,5},{5,6},{6,7},{7,8},{8,9},{9,10... | collective-permute-start | bytes 1769480 | tf_op jit(solution)/shard_map/ppermute | solution.py:13
  22.8 183.5 %collective-permute-start.3 = (f32[256,1152]{1,0:T(8,128)S(1)}, f32[256,1152]{1,0:T(8,128)S(1)}, u32[]{:S(2)}, u32[]{:S(2)}) collective-permute-start(f32[256,1152]{1,0:T(8,128)S(1)} %fusion.9), channel_id=1, source_target_pairs={{63,0},{0,1},{1,2},{2,3},{3,4},{4,5},{5,6},{6,7},{7,8},{8,9},{9,10... | collective-permute-start | bytes 3538952 | tf_op jit(solution)/shard_map/ppermute | solution.py:13
  112.9 95.8 %collective-permute-start.6 = (f32[256,1152]{1,0:T(8,128)S(1)}, f32[256,1152]{1,0:T(8,128)S(1)}, u32[]{:S(2)}, u32[]{:S(2)}) collective-permute-start(f32[256,1152]{1,0:T(8,128)S(1)} %convolution_add_fusion), channel_id=1, source_target_pairs={{1,0},{2,1},{3,2},{4,3},{5,4},{6,5},{7,6},{8,7},{9,8},{10,9},{11,1... | collective-permute-start | bytes 3538952 | tf_op jit(solution)/shard_map/ppermute | solution.py:13
  114.8 91.0 %collective-permute-start = (bf16[256,1152]{1,0:T(8,128)(2,1)S(1)}, bf16[256,1152]{1,0:T(8,128)(2,1)S(1)}, u32[]{:S(2)}, u32[]{:S(2)}) collective-permute-start(bf16[256,1152]{1,0:T(8,128)(2,1)S(1)} %convert_element_type.22), channel_id=1, source_target_pairs={{63,0},{0,1},{1,2},{2,3},{3,4},{4,5},{5,6},{6,7},{7,8},{8,9},{9,10... | collective-permute-start | bytes 1769480 | tf_op jit(solution)/shard_map/ppermute | solution.py:13
  206.7 22.3 %collective-permute-start.4 = (f32[256,1152]{1,0:T(8,128)S(1)}, f32[256,1152]{1,0:T(8,128)S(1)}, u32[]{:S(2)}, u32[]{:S(2)}) collective-permute-start(f32[256,1152]{1,0:T(8,128)S(1)} %convolution_add_fusion.1), channel_id=1, source_target_pairs={{1,0},{2,1},{3,2},{4,3},{5,4},{6,5},{7,6},{8,7},{9,8},{10,9},{11,1... | collective-permute-start | bytes 3538952 | tf_op jit(solution)/shard_map/ppermute | solution.py:13
  208.7 111.9 %collective-permute-start.7 = (f32[256,1152]{1,0:T(8,128)S(1)}, f32[256,1152]{1,0:T(8,128)S(1)}, u32[]{:S(2)}, u32[]{:S(2)}) collective-permute-start(f32[256,1152]{1,0:T(8,128)S(1)} %collective-permute-done.6), channel_id=1, source_target_pairs={{64,0},{128,64},{192,128},{256,192},{320,256},{384,320},{448,384},... | collective-permute-start | bytes 3538952 | tf_op jit(solution)/shard_map/ppermute | solution.py:13
where the time goes:
time: 322 us
  waiting for transfers between devices  279 us (87%)
  starting transfers between devices  31.5 us (10%)
  matrix products  6.16 us (2%)
    ppermute x8, waiting for transfers between devices, shifted(): return lax.ppermute(block, axis, route)  279 us
    ppermute x8, starting transfers between devices, shifted(): return lax.ppermute(block, axis, route)  31.5 us
  transfers between devices with their start and end apart: 8, of which 5 were waited for; matrix products, arithmetic and copies ran while one was open for 2% of the time, Pallas kernels for 0%

commit v1 on v0

v1 whole, which is shorter than its diff:
```python
import functools

import jax
import jax.numpy as jnp
from jax import lax
from jax.experimental import pallas as pl
from jax.experimental.pallas import tpu as pltpu
from jax.sharding import PartitionSpec as P

INNER_STEPS = 2
OUTER_STEPS = 2
MESH = pl.DeviceIdType.MESH

CHUNKS = 4
PIECES = 16
UNITS = 2

TEXT_ROUTE = (24, 16, 8, 7, 24, 16, 8, 15, 24, 16, 8, 25, 31, 23, 25, 17)
IMAGE_ROUTE = tuple(31 - column for column in TEXT_ROUTE)


def either(*conditions):
    return functools.reduce(jnp.logical_or, conditions)


def kernel(
    scale_ref, bias_ref, image_hbm, text_hbm, grad_image_hbm, grad_text_hbm, loss_ref,
    image_f32, text_f32, own_image, own_text, images, texts, relay_image, relay_text,
    acc_image, acc_text, load_sem, store_sem, send_sem, relay_send_image, relay_send_text,
    recv_image, recv_text, recv_relay_image, recv_relay_text,
):
    outer, inner = lax.axis_index("outer"), lax.axis_index("inner")
    n_outer, n_inner = lax.axis_size("outer"), lax.axis_size("inner")
    half_size = n_inner // 2
    last = half_size - 1
    rows, width = own_image.shape
    chunk, piece, unit = rows // CHUNKS, rows // PIECES, rows // UNITS
    per_chunk = PIECES // CHUNKS

    half, column = lax.div(inner, half_size), lax.rem(inner, half_size)
    first_core = lax.rem(outer, 2) == 0
    is_last, is_first = column == last, column == 0
    not_last, not_first = column != last, column != 0
    here, there = half * half_size, (1 - half) * half_size
    up = (outer, lax.rem(inner + 1, n_inner))
    down = (outer, lax.rem(inner + n_inner - 1, n_inner))
    ahead = (lax.rem(outer + 1, n_outer), inner)
    behind = (lax.rem(outer + n_outer - 1, n_outer), inner)

    text_columns = sorted(set(TEXT_ROUTE))
    image_columns = sorted(set(IMAGE_ROUTE))

    loads = []
    for c in range(CHUNKS):
        part = pl.ds(c * chunk, chunk)
        for k, (source, target) in enumerate(((text_hbm, text_f32), (image_hbm, image_f32))):
            load = pltpu.make_async_copy(source.at[part], target.at[part], load_sem.at[k, c])
            load.start()
            loads.append(load)

    barrier = pltpu.get_barrier_semaphore()

    def greet(device):
        pl.semaphore_signal(barrier, inc=1, device_id=device, device_id_type=MESH)

    greet(ahead)
    greet(behind)

    @pl.when(not_last)
    def _():
        greet(up)

    @pl.when(not_first)
    def _():
        greet(down)

    @pl.when(is_last)
    def _():
        for c in image_columns:
            greet((outer, there + c))

    @pl.when(is_first)
    def _():
        for c in text_columns:
            greet((outer, there + c))

    relays_text = either(*[column == c for c in text_columns if c != last])
    relays_image = either(*[column == c for c in image_columns if c != 0])

    @pl.when(relays_text)
    def _():
        greet((outer, here + last))

    @pl.when(relays_image)
    def _():
        greet((outer, here))

    def as_rows(k, c):
        loads[2 * c + k].wait()
        part = pl.ds(c * chunk, chunk)
        if k == 0:
            own_text[part] = text_f32[part].astype(jnp.bfloat16)
        else:
            own_image[part] = image_f32[part].astype(jnp.bfloat16)

    as_rows(0, 0)
    as_rows(1, 0)

    peers = {}
    for c in range(half_size):
        count = 2 + (c != last) + (c != 0)
        count += len(text_columns) if c == last else c in text_columns
        count += len(image_columns) if c == 0 else c in image_columns
        peers.setdefault(count, []).append(c)
    for count, columns in peers.items():

        @pl.when(either(*[column == c for c in columns]))
        def _():
            pl.semaphore_wait(barrier, count)

    def send(source, target, sent, received, device):
        pltpu.make_async_remote_copy(
            src_ref=source, dst_ref=target, send_sem=sent, recv_sem=received,
            device_id=device, device_id_type=MESH,
        ).start()

    def arrived(target, received):
        pltpu.make_async_remote_copy(
            src_ref=target, dst_ref=target, send_sem=send_sem.at[0], recv_sem=received,
            device_id=ahead, device_id_type=MESH,
        ).wait_recv()

    def left(source, sent):
        pltpu.make_async_remote_copy(
            src_ref=source, dst_ref=source, send_sem=sent, recv_sem=recv_text.at[0, 0],
            device_id=ahead, device_id_type=MESH,
        ).wait_send()

    for c in range(CHUNKS):
        part = pl.ds(c * chunk, chunk)
        if c > 0:
            as_rows(0, c)
        send(own_text.at[part], texts.at[0, part], send_sem.at[0], recv_text.at[0, c], ahead)

        @pl.when(not_last)
        def _():
            send(own_text.at[part], texts.at[1, part], send_sem.at[1], recv_text.at[1, c], up)

        @pl.when(is_last)
        def _():
            for p in range(c * per_chunk, (c + 1) * per_chunk):
                bit = pl.ds(p * piece, piece)
                via = TEXT_ROUTE[p]
                if via == last:
                    send(own_text.at[bit], texts.at[1, bit], send_sem.at[1], recv_text.at[1, c], (outer, there))
                else:
                    send(own_text.at[bit], relay_text.at[bit], send_sem.at[1], recv_relay_text.at[p],
                         (outer, here + via))

        if c > 0:
            as_rows(1, c)
        send(own_image.at[part], images.at[0, part], send_sem.at[2], recv_image.at[0, c], behind)

        @pl.when(not_first)
        def _():
            send(own_image.at[part], images.at[1, part], send_sem.at[3], recv_image.at[1, c], down)

        @pl.when(is_first)
        def _():
            for p in range(c * per_chunk, (c + 1) * per_chunk):
                bit = pl.ds(p * piece, piece)
                via = IMAGE_ROUTE[p]
                if via == 0:
                    send(own_image.at[bit], images.at[1, bit], send_sem.at[3], recv_image.at[1, c],
                         (outer, there + last))
                else:
                    send(own_image.at[bit], relay_image.at[bit], send_sem.at[3], recv_relay_image.at[p],
                         (outer, here + via))

    scale, bias = scale_ref[0], bias_ref[0]
    tiles = [pl.ds(k * (width // 3), width // 3) for k in range(3)]

    def logits(mine, theirs):
        return scale * lax.dot_general(
            mine, theirs, (((1,), (1,)), ((), ())), preferred_element_type=jnp.float32
        ) + bias

    def sigmoid_and_tail(score):
        small = jnp.exp(-jnp.abs(score))
        share = 1.0 / (1.0 + small)
        return jnp.where(score >= 0, share, small * share), small

    def add_image(theirs, target, start):
        score = logits(own_image[...], theirs)
        positive, small = sigmoid_and_tail(score)
        if target:
            row = lax.broadcasted_iota(jnp.int32, score.shape, 0)
            col = lax.broadcasted_iota(jnp.int32, score.shape, 1) + start
            wanted = row == col
            positive = jnp.where(wanted, positive - 1.0, positive)
            score = jnp.where(wanted, -score, score)
        weights = (scale * positive).astype(jnp.bfloat16)
        loss = jnp.sum(jnp.maximum(score, 0.0) + jnp.log1p(small), axis=1, keepdims=True)
        return weights, loss

    def add_text(theirs, target, start):
        score = logits(own_text[...], theirs)
        positive, _ = sigmoid_and_tail(score)
        if target:
            row = lax.broadcasted_iota(jnp.int32, score.shape, 0)
            col = lax.broadcasted_iota(jnp.int32, score.shape, 1) + start
            positive = jnp.where(row == col, positive - 1.0, positive)
        return (scale * positive).astype(jnp.bfloat16)

    def meet_text(block, u, losses, target=False, fresh=False):
        part = pl.ds(u * unit, unit)
        weights, loss = add_image(block[part], target, u * unit)
        for tile in tiles:
            term = jnp.dot(weights, block[part, tile], preferred_element_type=jnp.float32)
            acc_image[:, tile] = term if fresh else acc_image[:, tile] + term
        return losses + loss

    def meet_image(block, u, target=False, fresh=False):
        part = pl.ds(u * unit, unit)
        weights = add_text(block[part], target, u * unit)
        for tile in tiles:
            term = jnp.dot(weights, block[part, tile], preferred_element_type=jnp.float32)
            acc_text[:, tile] = term if fresh else acc_text[:, tile] + term

    losses = jnp.zeros((rows, 1), jnp.float32)
    for u in range(UNITS):
        losses = meet_text(own_text, u, losses, target=True, fresh=u == 0)
        meet_image(own_image, u, target=True, fresh=u == 0)

    def pass_pieces(c):
        for p in range(c * per_chunk, (c + 1) * per_chunk):
            bit = pl.ds(p * piece, piece)
            if TEXT_ROUTE[p] != last:

                @pl.when(column == TEXT_ROUTE[p])
                def _():
                    arrived(relay_text.at[bit], recv_relay_text.at[p])
                    send(relay_text.at[bit], texts.at[1, bit], relay_send_text.at[p], recv_text.at[1, c],
                         (outer, there))

            if IMAGE_ROUTE[p] != 0:

                @pl.when(column == IMAGE_ROUTE[p])
                def _():
                    arrived(relay_image.at[bit], recv_relay_image.at[p])
                    send(relay_image.at[bit], images.at[1, bit], relay_send_image.at[p], recv_image.at[1, c],
                         (outer, there + last))

    def pass_text(c):
        part = pl.ds(c * chunk, chunk)
        arrived(texts.at[1, part], recv_text.at[1, c])

        @pl.when(jnp.logical_or(first_core, is_first))
        def _():
            send(texts.at[1, part], texts.at[2, part], send_sem.at[6], recv_text.at[2, c], ahead)

    def pass_image(c):
        part = pl.ds(c * chunk, chunk)
        arrived(images.at[1, part], recv_image.at[1, c])

        @pl.when(jnp.logical_or(jnp.logical_not(first_core), is_last))
        def _():
            send(images.at[1, part], images.at[2, part], send_sem.at[7], recv_image.at[2, c], behind)

    per_unit = CHUNKS // UNITS
    pass_pieces(0)
    for c in range(CHUNKS):
        part = pl.ds(c * chunk, chunk)
        if c + 1 < CHUNKS:
            pass_pieces(c + 1)
        arrived(texts.at[0, part], recv_text.at[0, c])

        @pl.when(jnp.logical_and(first_core, not_last))
        def _():
            send(texts.at[0, part], texts.at[2, part], send_sem.at[4], recv_text.at[2, c], up)

        arrived(images.at[0, part], recv_image.at[0, c])

        @pl.when(jnp.logical_and(jnp.logical_not(first_core), not_first))
        def _():
            send(images.at[0, part], images.at[2, part], send_sem.at[5], recv_image.at[2, c], down)

        @pl.when(not_first)
        def _():
            pass_text(c)

        @pl.when(not_last)
        def _():
            pass_image(c)

        if (c + 1) % per_unit == 0:
            losses = meet_text(texts.at[0], c // per_unit, losses)
            meet_image(images.at[0], c // per_unit)

    for u in range(UNITS):

        @pl.when(is_first)
        def _():
            for c in range(u * per_unit, (u + 1) * per_unit):
                pass_text(c)

        @pl.when(is_last)
        def _():
            for c in range(u * per_unit, (u + 1) * per_unit):
                pass_image(c)

        losses = meet_text(texts.at[1], u, losses)
        meet_image(images.at[1], u)

    for u in range(UNITS):
        for c in range(u * per_unit, (u + 1) * per_unit):
            part = pl.ds(c * chunk, chunk)
            arrived(texts.at[2, part], recv_text.at[2, c])
        losses = meet_text(texts.at[2], u, losses)
        if u == UNITS - 1:
            stores = [pltpu.make_async_copy(acc_image, grad_image_hbm, store_sem.at[0])]
            stores[0].start()
        for c in range(u * per_unit, (u + 1) * per_unit):
            part = pl.ds(c * chunk, chunk)
            arrived(images.at[2, part], recv_image.at[2, c])
        meet_image(images.at[2], u)
    stores.append(pltpu.make_async_copy(acc_text, grad_text_hbm, store_sem.at[1]))
    stores[1].start()
    loss_ref[...] = losses / (OUTER_STEPS * INNER_STEPS * rows)

    for k, block in ((0, own_text), (1, own_text), (2, own_image), (3, own_image)):
        left(block, send_sem.at[k])

    @pl.when(jnp.logical_and(first_core, not_last))
    def _():
        left(texts.at[0], send_sem.at[4])

    @pl.when(jnp.logical_and(jnp.logical_not(first_core), not_first))
    def _():
        left(images.at[0], send_sem.at[5])

    @pl.when(jnp.logical_or(first_core, is_first))
    def _():
        left(texts.at[1], send_sem.at[6])

    @pl.when(jnp.logical_or(jnp.logical_not(first_core), is_last))
    def _():
        left(images.at[1], send_sem.at[7])

    for p in range(PIECES):
        bit = pl.ds(p * piece, piece)
        if TEXT_ROUTE[p] != last:

            @pl.when(column == TEXT_ROUTE[p])
            def _():
                left(relay_text.at[bit], relay_send_text.at[p])

        if IMAGE_ROUTE[p] != 0:

            @pl.when(column == IMAGE_ROUTE[p])
            def _():
                left(relay_image.at[bit], relay_send_image.at[p])

    for store in stores:
        store.wait()


def per_device(image_emb, text_emb, score_scale, logit_bias):
    rows, width = image_emb.shape
    smem = pl.BlockSpec(memory_space=pltpu.SMEM)
    hbm = pl.BlockSpec(memory_space=pl.ANY)
    grad = jax.ShapeDtypeStruct((rows, width), jnp.float32)
    narrow, wide = pltpu.VMEM((rows, width), jnp.bfloat16), pltpu.VMEM((rows, width), jnp.float32)
    dma = pltpu.SemaphoreType.DMA
    grad_image, grad_text, row_loss = pl.pallas_call(
        kernel,
        out_shape=(grad, grad, jax.ShapeDtypeStruct((rows, 1), jnp.float32)),
        in_specs=[smem, smem, hbm, hbm],
        out_specs=(hbm, hbm, pl.BlockSpec(memory_space=pltpu.VMEM)),
        scratch_shapes=[
            wide, wide, narrow, narrow,
            pltpu.VMEM((3, rows, width), jnp.bfloat16),
            pltpu.VMEM((3, rows, width), jnp.bfloat16),
            narrow, narrow, wide, wide,
            dma((2, CHUNKS)), dma((2,)), dma((8,)), dma((PIECES,)), dma((PIECES,)),
            dma((3, CHUNKS)), dma((3, CHUNKS)), dma((PIECES,)), dma((PIECES,)),
        ],
        compiler_params=pltpu.CompilerParams(
            collective_id=0, has_side_effects=True, vmem_limit_bytes=48 * 2**20
        ),
    )(score_scale, logit_bias, image_emb, text_emb)
    return grad_image, grad_text, row_loss[:, 0]


def solution(mesh):
    return jax.shard_map(
        per_device,
        mesh=mesh,
        in_specs=(P(("outer", "inner"), None), P(("outer", "inner"), None), P(), P()),
        out_specs=(P(("outer", "inner"), None), P(("outer", "inner"), None), P(("outer", "inner"))),
        check_vma=False,
    )
```

time: 322 us -> 59.6 us (0.19)
  the two profiles are of different devices: /device:TPU:193 before, /device:TPU:384 now
where the time goes in v1:
time: 59.6 us; the launch traced here: 59.4 us
  Pallas kernels  52.2 us (88%)
  local copies, waits for them, and re-layouts  4.56 us (8%)
  between operations  1.94 us (3%)
  other arithmetic  0.68 us (1%)
    pallas_call x1, Pallas kernels, per_device(): pl.pallas_call(kernel, out_shape=(grad, grad, jax.ShapeDtypeStruct((rows,...  52.2 us
    unnamed x6, local copies, waits for them, and re-layouts  4.56 us

profile of v1, /device:TPU:384, one launch (start us, length us, event | category | flops | bytes accessed | tf_op | source)
XLA Modules:
  0.0 59.4 jit_solution(5441213480814708668)
XLA Ops:
  1.9 0.0 copy-start
  1.9 1.3 %copy-done = f32[256,1152]{1,0:T(8,128)S(1)} copy-done((f32[256,1152]{1,0:T(8,128)S(1)}, f32[256,1152]{1,0:T(8,128)}, u32[]{:S(2)}) %copy-start) | copy-done | bytes 1179672
  3.2 0.0 copy-start.1
  3.2 1.3 %copy-done.1 = f32[256,1152]{1,0:T(8,128)S(1)} copy-done((f32[256,1152]{1,0:T(8,128)S(1)}, f32[256,1152]{1,0:T(8,128)}, u32[]{:S(2)}) %copy-start.1) | copy-done | bytes 1179672
  4.5 52.2 %shard_map.67 = (f32[256,1152]{1,0:T(8,128)S(1)}, f32[256,1152]{1,0:T(8,128)S(1)}, f32[256,1]{1,0:T(8,128)S(1)}) custom-call(f32[1]{0:T(128)S(6)} %copy.9.scale_ref, f32[1]{0:T(128)S(6)} %copy.10.bias_ref, f32[256,1152]{1,0:T(8,128)S(1)} %copy-done, f32[256,1152]{1,0:T(8,128)S(1)} %copy-done.1), custom_call_target="tpu_custom_call" | custom-call | tf_op jit(solution)/shard_map/pallas_call | solution.py:375
  56.7 0.7 %reduce = f32[256]{0:T(256)} reduce(f32[256,1]{1,0:T(8,128)S(1)} %get-tuple-element.8, f32[]{:T(128)} %constant.2), dimensions={1}, to_apply=%get-tuple-element.8.reduce_sub_computation | reduce | bytes 2052 | tf_op jit(solution)/shard_map/pallas_call | solution.py:375
  57.4 1.0 %copy.11 = f32[256,1152]{1,0:T(8,128)} copy(f32[256,1152]{1,0:T(8,128)S(1)} %get-tuple-element.12) | data formatting | bytes 2359296
  58.4 1.0 %copy.12 = f32[256,1152]{1,0:T(8,128)} copy(f32[256,1152]{1,0:T(8,128)S(1)} %get-tuple-element.13) | data formatting | bytes 2359296
Async XLA Ops:
  1.9 1.3 %copy-start = (f32[256,1152]{1,0:T(8,128)S(1)}, f32[256,1152]{1,0:T(8,128)}, u32[]{:S(2)}) copy-start(f32[256,1152]{1,0:T(8,128)} %image_hbm.1) | copy-start | bytes 3538948
  3.2 1.3 %copy-start.1 = (f32[256,1152]{1,0:T(8,128)S(1)}, f32[256,1152]{1,0:T(8,128)}, u32[]{:S(2)}) copy-start(f32[256,1152]{1,0:T(8,128)} %text_hbm.1) | copy-start | bytes 3538948

commit v2 on v1

--- a/solution.py
+++ b/solution.py
@@ -15,7 +15,7 @@
 PIECES = 16
 UNITS = 2
 
-TEXT_ROUTE = (24, 16, 8, 7, 24, 16, 8, 15, 24, 16, 8, 25, 31, 23, 25, 17)
+TEXT_ROUTE = (24, 16, 8, 1, 24, 16, 8, 6, 24, 16, 8, 14, 17, 9, 1, 6)
 IMAGE_ROUTE = tuple(31 - column for column in TEXT_ROUTE)
 
 
@@ -24,10 +24,10 @@
 
 
 def kernel(
-    scale_ref, bias_ref, image_hbm, text_hbm, grad_image_hbm, grad_text_hbm, loss_ref,
+    scale_ref, bias_ref, image_hbm, text_hbm, acc_image, acc_text, loss_ref,
     image_f32, text_f32, own_image, own_text, images, texts, relay_image, relay_text,
-    acc_image, acc_text, load_sem, store_sem, send_sem, relay_send_image, relay_send_text,
-    recv_image, recv_text, recv_relay_image, recv_relay_text,
+    pair_losses, load_sem, send_sem, relay_send_image, relay_send_text,
+    recv_image, recv_text, recv_relay_image, recv_relay_text, ready_image, ready_text,
 ):
     outer, inner = lax.axis_index("outer"), lax.axis_index("inner")
     n_outer, n_inner = lax.axis_size("outer"), lax.axis_size("inner")
@@ -74,26 +74,35 @@
     def _():
         greet(down)
 
-    @pl.when(is_last)
+    early = half == 0
+    relays_text = either(*[column == c for c in text_columns])
+    relays_image = either(*[column == c for c in image_columns])
+
+    @pl.when(jnp.logical_and(is_last, early))
     def _():
         for c in image_columns:
             greet((outer, there + c))
 
-    @pl.when(is_first)
+    @pl.when(jnp.logical_and(is_first, early))
     def _():
         for c in text_columns:
             greet((outer, there + c))
 
-    relays_text = either(*[column == c for c in text_columns if c != last])
-    relays_image = either(*[column == c for c in image_columns if c != 0])
-
     @pl.when(relays_text)
     def _():
         greet((outer, here + last))
 
+        @pl.when(early)
+        def _():
+            greet((outer, there))
+
     @pl.when(relays_image)
     def _():
         greet((outer, here))
+
+        @pl.when(early)
+        def _():
+            greet((outer, there + last))
 
     def as_rows(k, c):
         loads[2 * c + k].wait()
@@ -107,16 +116,27 @@
     as_rows(1, 0)
 
     peers = {}
-    for c in range(half_size):
+    for i in range(n_inner):
+        late, c = divmod(i, half_size)
         count = 2 + (c != last) + (c != 0)
-        count += len(text_columns) if c == last else c in text_columns
-        count += len(image_columns) if c == 0 else c in image_columns
-        peers.setdefault(count, []).append(c)
-    for count, columns in peers.items():
-
-        @pl.when(either(*[column == c for c in columns]))
+        count += (1 + late) * len(text_columns) if c == last else late * (c in text_columns)
+        count += (1 + late) * len(image_columns) if c == 0 else late * (c in image_columns)
+        peers.setdefault(count, []).append(i)
+    for count, places in peers.items():
+
+        @pl.when(either(*[inner == i for i in places]))
         def _():
             pl.semaphore_wait(barrier, count)
+
+    @pl.when(jnp.logical_and(is_last, jnp.logical_not(early)))
+    def _():
+        for c in image_columns:
+            pl.semaphore_signal(ready_image, inc=1, device_id=(outer, there + c), device_id_type=MESH)
+
+    @pl.when(jnp.logical_and(is_first, jnp.logical_not(early)))
+    def _():
+        for c in text_columns:
+            pl.semaphore_signal(ready_text, inc=1, device_id=(outer, there + c), device_id_type=MESH)
 
     def send(source, target, sent, received, device):
         pltpu.make_async_remote_copy(
@@ -151,11 +171,8 @@
             for p in range(c * per_chunk, (c + 1) * per_chunk):
                 bit = pl.ds(p * piece, piece)
                 via = TEXT_ROUTE[p]
-                if via == last:
-                    send(own_text.at[bit], texts.at[1, bit], send_sem.at[1], recv_text.at[1, c], (outer, there))
-                else:
-                    send(own_text.at[bit], relay_text.at[bit], send_sem.at[1], recv_relay_text.at[p],
-                         (outer, here + via))
+                send(own_text.at[bit], relay_text.at[bit], send_sem.at[1], recv_relay_text.at[p],
+                     (outer, here + via))
 
         if c > 0:
             as_rows(1, c)
@@ -170,12 +187,31 @@
             for p in range(c * per_chunk, (c + 1) * per_chunk):
                 bit = pl.ds(p * piece, piece)
                 via = IMAGE_ROUTE[p]
-                if via == 0:
-                    send(own_image.at[bit], images.at[1, bit], send_sem.at[3], recv_image.at[1, c],
-                         (outer, there + last))
-                else:
-                    send(own_image.at[bit], relay_image.at[bit], send_sem.at[3], recv_relay_image.at[p],
-                         (outer, here + via))
+                send(own_image.at[bit], relay_image.at[bit], send_sem.at[3], recv_relay_image.at[p],
+                     (outer, here + via))
+
+    @pl.when(jnp.logical_and(relays_text, early))
+    def _():
+        pl.semaphore_wait(ready_text, 1)
+
+    @pl.when(jnp.logical_and(relays_image, early))
+    def _():
+        pl.semaphore_wait(ready_image, 1)
+
+    for p in range(PIECES):
+        c = p // per_chunk
+        bit = pl.ds(p * piece, piece)
+
+        @pl.when(column == TEXT_ROUTE[p])
+        def _():
+            arrived(relay_text.at[bit], recv_relay_text.at[p])
+            send(relay_text.at[bit], texts.at[1, bit], relay_send_text.at[p], recv_text.at[1, c], (outer, there))
+
+        @pl.when(column == IMAGE_ROUTE[p])
+        def _():
+            arrived(relay_image.at[bit], recv_relay_image.at[p])
+            send(relay_image.at[bit], images.at[1, bit], relay_send_image.at[p], recv_image.at[1, c],
+                 (outer, there + last))
 
     scale, bias = scale_ref[0], bias_ref[0]
     tiles = [pl.ds(k * (width // 3), width // 3) for k in range(3)]
@@ -200,8 +236,7 @@
             positive = jnp.where(wanted, positive - 1.0, positive)
             score = jnp.where(wanted, -score, score)
         weights = (scale * positive).astype(jnp.bfloat16)
-        loss = jnp.sum(jnp.maximum(score, 0.0) + jnp.log1p(small), axis=1, keepdims=True)
-        return weights, loss
+        return weights, jnp.maximum(score, 0.0) + jnp.log1p(small)
 
     def add_text(theirs, target, start):
         score = logits(own_text[...], theirs)
@@ -212,13 +247,13 @@
             positive = jnp.where(row == col, positive - 1.0, positive)
         return (scale * positive).astype(jnp.bfloat16)
 
-    def meet_text(block, u, losses, target=False, fresh=False):
+    def meet_text(block, u, target=False, fresh=False):
         part = pl.ds(u * unit, unit)
         weights, loss = add_image(block[part], target, u * unit)
         for tile in tiles:
             term = jnp.dot(weights, block[part, tile], preferred_element_type=jnp.float32)
             acc_image[:, tile] = term if fresh else acc_image[:, tile] + term
-        return losses + loss
+        pair_losses[...] = loss if fresh else pair_losses[...] + loss
 
     def meet_image(block, u, target=False, fresh=False):
         part = pl.ds(u * unit, unit)
@@ -227,30 +262,10 @@
             term = jnp.dot(weights, block[part, tile], preferred_element_type=jnp.float32)
             acc_text[:, tile] = term if fresh else acc_text[:, tile] + term
 
-    losses = jnp.zeros((rows, 1), jnp.float32)
     for u in range(UNITS):
-        losses = meet_text(own_text, u, losses, target=True, fresh=u == 0)
+        meet_text(own_text, u, target=True, fresh=u == 0)
         meet_image(own_image, u, target=True, fresh=u == 0)
 
-    def pass_pieces(c):
-        for p in range(c * per_chunk, (c + 1) * per_chunk):
-            bit = pl.ds(p * piece, piece)
-            if TEXT_ROUTE[p] != last:
-
-                @pl.when(column == TEXT_ROUTE[p])
-                def _():
-                    arrived(relay_text.at[bit], recv_relay_text.at[p])
-                    send(relay_text.at[bit], texts.at[1, bit], relay_send_text.at[p], recv_text.at[1, c],
-                         (outer, there))
-
-            if IMAGE_ROUTE[p] != 0:
-
-                @pl.when(column == IMAGE_ROUTE[p])
-                def _():
-                    arrived(relay_image.at[bit], recv_relay_image.at[p])
-                    send(relay_image.at[bit], images.at[1, bit], relay_send_image.at[p], recv_image.at[1, c],
-                         (outer, there + last))
-
     def pass_text(c):
         part = pl.ds(c * chunk, chunk)
         arrived(texts.at[1, part], recv_text.at[1, c])
@@ -268,11 +283,8 @@
             send(images.at[1, part], images.at[2, part], send_sem.at[7], recv_image.at[2, c], behind)
 
     per_unit = CHUNKS // UNITS
-    pass_pieces(0)
     for c in range(CHUNKS):
         part = pl.ds(c * chunk, chunk)
-        if c + 1 < CHUNKS:
-            pass_pieces(c + 1)
         arrived(texts.at[0, part], recv_text.at[0, c])
 
         @pl.when(jnp.logical_and(first_core, not_last))
@@ -294,7 +306,7 @@
             pass_image(c)
 
         if (c + 1) % per_unit == 0:
-            losses = meet_text(texts.at[0], c // per_unit, losses)
+            meet_text(texts.at[0], c // per_unit)
             meet_image(images.at[0], c // per_unit)
 
     for u in range(UNITS):
@@ -309,24 +321,20 @@
             for c in range(u * per_unit, (u + 1) * per_unit):
                 pass_image(c)
 
-        losses = meet_text(texts.at[1], u, losses)
+        meet_text(texts.at[1], u)
         meet_image(images.at[1], u)
 
     for u in range(UNITS):
         for c in range(u * per_unit, (u + 1) * per_unit):
             part = pl.ds(c * chunk, chunk)
             arrived(texts.at[2, part], recv_text.at[2, c])
-        losses = meet_text(texts.at[2], u, losses)
-        if u == UNITS - 1:
-            stores = [pltpu.make_async_copy(acc_image, grad_image_hbm, store_sem.at[0])]
-            stores[0].start()
+        meet_text(texts.at[2], u)
         for c in range(u * per_unit, (u + 1) * per_unit):
             part = pl.ds(c * chunk, chunk)
             arrived(images.at[2, part], recv_image.at[2, c])
         meet_image(images.at[2], u)
-    stores.append(pltpu.make_async_copy(acc_text, grad_text_hbm, store_sem.at[1]))
-    stores[1].start()
-    loss_ref[...] = losses / (OUTER_STEPS * INNER_STEPS * rows)
+    row_losses = jnp.sum(jnp.transpose(pair_losses[...]), axis=0, keepdims=True)
+    loss_ref[...] = row_losses / (OUTER_STEPS * INNER_STEPS * rows)
 
     for k, block in ((0, own_text), (1, own_text), (2, own_image), (3, own_image)):
         left(block, send_sem.at[k])
@@ -349,47 +357,41 @@
 
     for p in range(PIECES):
         bit = pl.ds(p * piece, piece)
-        if TEXT_ROUTE[p] != last:
-
-            @pl.when(column == TEXT_ROUTE[p])
-            def _():
-                left(relay_text.at[bit], relay_send_text.at[p])
-
-        if IMAGE_ROUTE[p] != 0:
-
-            @pl.when(column == IMAGE_ROUTE[p])
-            def _():
-                left(relay_image.at[bit], relay_send_image.at[p])
-
-    for store in stores:
-        store.wait()
+
+        @pl.when(column == TEXT_ROUTE[p])
+        def _():
+            left(relay_text.at[bit], relay_send_text.at[p])
+
+        @pl.when(column == IMAGE_ROUTE[p])
+        def _():
+            left(relay_image.at[bit], relay_send_image.at[p])
 
 
 def per_device(image_emb, text_emb, score_scale, logit_bias):
     rows, width = image_emb.shape
     smem = pl.BlockSpec(memory_space=pltpu.SMEM)
-    hbm = pl.BlockSpec(memory_space=pl.ANY)
+    hbm, vmem = pl.BlockSpec(memory_space=pltpu.HBM), pl.BlockSpec(memory_space=pltpu.VMEM)
     grad = jax.ShapeDtypeStruct((rows, width), jnp.float32)
     narrow, wide = pltpu.VMEM((rows, width), jnp.bfloat16), pltpu.VMEM((rows, width), jnp.float32)
+    three = pltpu.VMEM((3, rows, width), jnp.bfloat16)
     dma = pltpu.SemaphoreType.DMA
     grad_image, grad_text, row_loss = pl.pallas_call(
         kernel,
-        out_shape=(grad, grad, jax.ShapeDtypeStruct((rows, 1), jnp.float32)),
+        out_shape=(grad, grad, jax.ShapeDtypeStruct((1, rows), jnp.float32)),
         in_specs=[smem, smem, hbm, hbm],
-        out_specs=(hbm, hbm, pl.BlockSpec(memory_space=pltpu.VMEM)),
+        out_specs=(vmem, vmem, vmem),
         scratch_shapes=[
-            wide, wide, narrow, narrow,
-            pltpu.VMEM((3, rows, width), jnp.bfloat16),
-            pltpu.VMEM((3, rows, width), jnp.bfloat16),
-            narrow, narrow, wide, wide,
-            dma((2, CHUNKS)), dma((2,)), dma((8,)), dma((PIECES,)), dma((PIECES,)),
+            wide, wide, narrow, narrow, three, three, narrow, narrow,
+            pltpu.VMEM((rows, rows // UNITS), jnp.float32),
+            dma((2, CHUNKS)), dma((8,)), dma((PIECES,)), dma((PIECES,)),
             dma((3, CHUNKS)), dma((3, CHUNKS)), dma((PIECES,)), dma((PIECES,)),
+            pltpu.SemaphoreType.REGULAR, pltpu.SemaphoreType.REGULAR,
         ],
         compiler_params=pltpu.CompilerParams(
-            collective_id=0, has_side_effects=True, vmem_limit_bytes=48 * 2**20
+            collective_id=0, has_side_effects=True, vmem_limit_bytes=51 * 2**20
         ),
     )(score_scale, logit_bias, image_emb, text_emb)
-    return grad_image, grad_text, row_loss[:, 0]
+    return grad_image, grad_text, row_loss[0]
 
 
 def solution(mesh):

time: 59.6 us -> 51.8 us (0.87)
  the two profiles are of different devices: /device:TPU:384 before, /device:TPU:1 now
where the time goes in v2:
time: 51.8 us; the launch traced here: 51.7 us
  Pallas kernels  47.1 us (91%)
  local copies, waits for them, and re-layouts  2.59 us (5%)
  between operations  1.93 us (4%)
    pallas_call x1, Pallas kernels, per_device(): pl.pallas_call(kernel, out_shape=(grad, grad, jax.ShapeDtypeStruct((1, ro...  47.1 us
    unnamed x3, local copies, waits for them, and re-layouts  2.59 us

profile of v2, /device:TPU:1, one launch (start us, length us, event | category | flops | bytes accessed | tf_op | source)
XLA Modules:
  0.0 51.7 jit_solution(14907310023710409686)
XLA Ops:
  1.9 47.1 %shard_map.67 = (f32[256,1152]{1,0:T(8,128)S(1)}, f32[256,1152]{1,0:T(8,128)S(1)}, f32[1,256]{1,0:T(1,128)S(1)}) custom-call(f32[1]{0:T(128)S(6)} %copy.10.scale_ref, f32[1]{0:T(128)S(6)} %copy.11.bias_ref, f32[256,1152]{1,0:T(8,128)} %image_hbm.1, f32[256,1152]{1,0:T(8,128)} %text_hbm.1), custom_call_target="tpu_custom_call" | custom-call | tf_op jit(solution)/shard_map/pallas_call | solution.py:378
  49.1 1.0 %copy.12 = f32[256,1152]{1,0:T(8,128)} copy(f32[256,1152]{1,0:T(8,128)S(1)} %get-tuple-element.12) | data formatting | bytes 2359296
  50.1 1.0 %copy.13 = f32[256,1152]{1,0:T(8,128)} copy(f32[256,1152]{1,0:T(8,128)S(1)} %get-tuple-element.13) | data formatting | bytes 2359296
  51.1 0.6 %copy.14 = f32[256]{0:T(256)} copy(f32[256]{0:T(256)S(1)} %bitcast.1) | data formatting | bytes 2048

commit v3 on v2

--- a/solution.py
+++ b/solution.py
@@ -16,6 +16,8 @@
 UNITS = 2
 
 TEXT_ROUTE = (24, 16, 8, 1, 24, 16, 8, 6, 24, 16, 8, 14, 17, 9, 1, 6)
+LATE_ORDER = (0, 1, -1, -2, -3, 2, 3, -4)
+ORDER = tuple(range(PIECES))
 IMAGE_ROUTE = tuple(31 - column for column in TEXT_ROUTE)
 
 
@@ -27,7 +29,8 @@
     scale_ref, bias_ref, image_hbm, text_hbm, acc_image, acc_text, loss_ref,
     image_f32, text_f32, own_image, own_text, images, texts, relay_image, relay_text,
     pair_losses, load_sem, send_sem, relay_send_image, relay_send_text,
-    recv_image, recv_text, recv_relay_image, recv_relay_text, ready_image, ready_text,
+    recv_image, recv_text, recv_relay_image, recv_relay_text,
+    recv_cross_image, recv_cross_text, ready_image, ready_text,
 ):
     outer, inner = lax.axis_index("outer"), lax.axis_index("inner")
     n_outer, n_inner = lax.axis_size("outer"), lax.axis_size("inner")
@@ -156,62 +159,77 @@
             device_id=ahead, device_id_type=MESH,
         ).wait_send()
 
-    for c in range(CHUNKS):
-        part = pl.ds(c * chunk, chunk)
-        if c > 0:
-            as_rows(0, c)
+    @pl.when(is_last)
+    def _():
+        for p in range(PIECES):
+            if p % per_chunk == 0 and p > 0:
+                as_rows(0, p // per_chunk)
+            bit = pl.ds(p * piece, piece)
+            send(own_text.at[bit], relay_text.at[bit], send_sem.at[1], recv_relay_text.at[p],
+                 (outer, here + TEXT_ROUTE[p]))
+
+    @pl.when(is_first)
+    def _():
+        for p in range(PIECES):
+            if p % per_chunk == 0 and p > 0:
+                as_rows(1, p // per_chunk)
+            bit = pl.ds(p * piece, piece)
+            send(own_image.at[bit], relay_image.at[bit], send_sem.at[3], recv_relay_image.at[p],
+                 (outer, here + IMAGE_ROUTE[p]))
+
+    def send_own(c):
+        part = pl.ds(c * chunk, chunk)
+
+        @pl.when(not_last)
+        def _():
+            if c > 0:
+                as_rows(0, c)
+            send(own_text.at[part], texts.at[1, part], send_sem.at[1], recv_text.at[1, c], up)
+
         send(own_text.at[part], texts.at[0, part], send_sem.at[0], recv_text.at[0, c], ahead)
 
-        @pl.when(not_last)
-        def _():
-            send(own_text.at[part], texts.at[1, part], send_sem.at[1], recv_text.at[1, c], up)
-
-        @pl.when(is_last)
-        def _():
-            for p in range(c * per_chunk, (c + 1) * per_chunk):
-                bit = pl.ds(p * piece, piece)
-                via = TEXT_ROUTE[p]
-                send(own_text.at[bit], relay_text.at[bit], send_sem.at[1], recv_relay_text.at[p],
-                     (outer, here + via))
-
-        if c > 0:
-            as_rows(1, c)
+        @pl.when(not_first)
+        def _():
+            if c > 0:
+                as_rows(1, c)
+            send(own_image.at[part], images.at[1, part], send_sem.at[3], recv_image.at[1, c], down)
+
         send(own_image.at[part], images.at[0, part], send_sem.at[2], recv_image.at[0, c], behind)
 
-        @pl.when(not_first)
-        def _():
-            send(own_image.at[part], images.at[1, part], send_sem.at[3], recv_image.at[1, c], down)
-
-        @pl.when(is_first)
-        def _():
-            for p in range(c * per_chunk, (c + 1) * per_chunk):
-                bit = pl.ds(p * piece, piece)
-                via = IMAGE_ROUTE[p]
-                send(own_image.at[bit], relay_image.at[bit], send_sem.at[3], recv_relay_image.at[p],
-                     (outer, here + via))
-
-    @pl.when(jnp.logical_and(relays_text, early))
-    def _():
-        pl.semaphore_wait(ready_text, 1)
-
-    @pl.when(jnp.logical_and(relays_image, early))
-    def _():
-        pl.semaphore_wait(ready_image, 1)
-
-    for p in range(PIECES):
-        c = p // per_chunk
-        bit = pl.ds(p * piece, piece)
-
-        @pl.when(column == TEXT_ROUTE[p])
-        def _():
-            arrived(relay_text.at[bit], recv_relay_text.at[p])
-            send(relay_text.at[bit], texts.at[1, bit], relay_send_text.at[p], recv_text.at[1, c], (outer, there))
-
-        @pl.when(column == IMAGE_ROUTE[p])
-        def _():
-            arrived(relay_image.at[bit], recv_relay_image.at[p])
-            send(relay_image.at[bit], images.at[1, bit], relay_send_image.at[p], recv_image.at[1, c],
-                 (outer, there + last))
+    def pass_pieces(c):
+        for p in range(c * per_chunk, (c + 1) * per_chunk):
+            bit = pl.ds(p * piece, piece)
+
+            @pl.when(column == TEXT_ROUTE[p])
+            def _():
+                arrived(relay_text.at[bit], recv_relay_text.at[p])
+                send(relay_text.at[bit], texts.at[1, bit], relay_send_text.at[p], recv_cross_text.at[p],
+                     (outer, there))
+
+            @pl.when(column == IMAGE_ROUTE[p])
+            def _():
+                arrived(relay_image.at[bit], recv_relay_image.at[p])
+                send(relay_image.at[bit], images.at[1, bit], relay_send_image.at[p], recv_cross_image.at[p],
+                     (outer, there + last))
+
+    for step in LATE_ORDER:
+        if step >= 0:
+            send_own(step)
+        else:
+            pl.when(jnp.logical_not(early))(functools.partial(pass_pieces, -1 - step))
+
+    @pl.when(early)
+    def _():
+        @pl.when(relays_text)
+        def _():
+            pl.semaphore_wait(ready_text, 1)
+
+        @pl.when(relays_image)
+        def _():
+            pl.semaphore_wait(ready_image, 1)
+
+        for c in range(CHUNKS):
+            pass_pieces(c)
 
     scale, bias = scale_ref[0], bias_ref[0]
     tiles = [pl.ds(k * (width // 3), width // 3) for k in range(3)]
@@ -270,7 +288,7 @@
         part = pl.ds(c * chunk, chunk)
         arrived(texts.at[1, part], recv_text.at[1, c])
 
-        @pl.when(jnp.logical_or(first_core, is_first))
+        @pl.when(first_core)
         def _():
             send(texts.at[1, part], texts.at[2, part], send_sem.at[6], recv_text.at[2, c], ahead)
 
@@ -278,9 +296,23 @@
         part = pl.ds(c * chunk, chunk)
         arrived(images.at[1, part], recv_image.at[1, c])
 
-        @pl.when(jnp.logical_or(jnp.logical_not(first_core), is_last))
+        @pl.when(jnp.logical_not(first_core))
         def _():
             send(images.at[1, part], images.at[2, part], send_sem.at[7], recv_image.at[2, c], behind)
+
+    def end_text():
+        for u in range(UNITS):
+            for c in range(u * per_unit, (u + 1) * per_unit):
+                part = pl.ds(c * chunk, chunk)
+                arrived(texts.at[2, part], recv_text.at[2, c])
+            meet_text(texts.at[2], u)
+
+    def end_image():
+        for u in range(UNITS):
+            for c in range(u * per_unit, (u + 1) * per_unit):
+                part = pl.ds(c * chunk, chunk)
+                arrived(images.at[2, part], recv_image.at[2, c])
+            meet_image(images.at[2], u)
 
     per_unit = CHUNKS // UNITS
     for c in range(CHUNKS):
@@ -309,30 +341,50 @@
             meet_text(texts.at[0], c // per_unit)
             meet_image(images.at[0], c // per_unit)
 
-    for u in range(UNITS):
-
-        @pl.when(is_first)
-        def _():
-            for c in range(u * per_unit, (u + 1) * per_unit):
-                pass_text(c)
-
-        @pl.when(is_last)
-        def _():
-            for c in range(u * per_unit, (u + 1) * per_unit):
-                pass_image(c)
-
-        meet_text(texts.at[1], u)
-        meet_image(images.at[1], u)
-
-    for u in range(UNITS):
-        for c in range(u * per_unit, (u + 1) * per_unit):
-            part = pl.ds(c * chunk, chunk)
-            arrived(texts.at[2, part], recv_text.at[2, c])
-        meet_text(texts.at[2], u)
-        for c in range(u * per_unit, (u + 1) * per_unit):
-            part = pl.ds(c * chunk, chunk)
-            arrived(images.at[2, part], recv_image.at[2, c])
-        meet_image(images.at[2], u)
+    @pl.when(not_first)
+    def _():
+        for u in range(UNITS):
+            meet_text(texts.at[1], u)
+
+    @pl.when(not_last)
+    def _():
+        for u in range(UNITS):
+            meet_image(images.at[1], u)
+
+    @pl.when(jnp.logical_and(is_first, early))
+    def _():
+        end_image()
+
+    @pl.when(is_first)
+    def _():
+        for p in ORDER:
+            bit = pl.ds(p * piece, piece)
+            arrived(texts.at[1, bit], recv_cross_text.at[p])
+            send(texts.at[1, bit], texts.at[2, bit], send_sem.at[6], recv_text.at[2, p // per_chunk], ahead)
+        for u in range(UNITS):
+            meet_text(texts.at[1], u)
+
+    @pl.when(jnp.logical_or(not_last, jnp.logical_not(early)))
+    def _():
+        end_text()
+
+    @pl.when(jnp.logical_and(is_last, early))
+    def _():
+        end_text()
+
+    @pl.when(is_last)
+    def _():
+        for p in ORDER:
+            bit = pl.ds(p * piece, piece)
+            arrived(images.at[1, bit], recv_cross_image.at[p])
+            send(images.at[1, bit], images.at[2, bit], send_sem.at[7], recv_image.at[2, p // per_chunk], behind)
+        for u in range(UNITS):
+            meet_image(images.at[1], u)
+
+    @pl.when(jnp.logical_or(not_first, jnp.logical_not(early)))
+    def _():
+        end_image()
+
     row_losses = jnp.sum(jnp.transpose(pair_losses[...]), axis=0, keepdims=True)
     loss_ref[...] = row_losses / (OUTER_STEPS * INNER_STEPS * rows)
 
@@ -385,7 +437,7 @@
             pltpu.VMEM((rows, rows // UNITS), jnp.float32),
             dma((2, CHUNKS)), dma((8,)), dma((PIECES,)), dma((PIECES,)),
             dma((3, CHUNKS)), dma((3, CHUNKS)), dma((PIECES,)), dma((PIECES,)),
-            pltpu.SemaphoreType.REGULAR, pltpu.SemaphoreType.REGULAR,
+            dma((PIECES,)), dma((PIECES,)), pltpu.SemaphoreType.REGULAR, pltpu.SemaphoreType.REGULAR,
         ],
         compiler_params=pltpu.CompilerParams(
             collective_id=0, has_side_effects=True, vmem_limit_bytes=51 * 2**20

time: 51.8 us -> 49.7 us (0.959)
  the two profiles are of different devices: /device:TPU:1 before, /device:TPU:255 now
where the time goes in v3:
time: 49.7 us; the launch traced here: 49.6 us
  Pallas kernels  45 us (91%)
  local copies, waits for them, and re-layouts  2.59 us (5%)
  between operations  1.93 us (4%)
    pallas_call x1, Pallas kernels, per_device(): pl.pallas_call(kernel, out_shape=(grad, grad, jax.ShapeDtypeStruct((1, ro...  45 us
    unnamed x3, local copies, waits for them, and re-layouts  2.59 us

profile of v3, /device:TPU:255, one launch (start us, length us, event | category | flops | bytes accessed | tf_op | source)
XLA Modules:
  0.0 49.6 jit_solution(8880442096520504912)
XLA Ops:
  1.9 45.0 %shard_map.67 = (f32[256,1152]{1,0:T(8,128)S(1)}, f32[256,1152]{1,0:T(8,128)S(1)}, f32[1,256]{1,0:T(1,128)S(1)}) custom-call(f32[1]{0:T(128)S(6)} %copy.10.scale_ref, f32[1]{0:T(128)S(6)} %copy.11.bias_ref, f32[256,1152]{1,0:T(8,128)} %image_hbm.1, f32[256,1152]{1,0:T(8,128)} %text_hbm.1), custom_call_target="tpu_custom_call" | custom-call | tf_op jit(solution)/shard_map/pallas_call | solution.py:430
  47.0 1.0 %copy.12 = f32[256,1152]{1,0:T(8,128)} copy(f32[256,1152]{1,0:T(8,128)S(1)} %get-tuple-element.12) | data formatting | bytes 2359296
  48.0 1.0 %copy.13 = f32[256,1152]{1,0:T(8,128)} copy(f32[256,1152]{1,0:T(8,128)S(1)} %get-tuple-element.13) | data formatting | bytes 2359296
  49.0 0.6 %copy.14 = f32[256]{0:T(256)} copy(f32[256]{0:T(256)S(1)} %bitcast.1) | data formatting | bytes 2048

commit v4 on v3

--- a/solution.py
+++ b/solution.py
@@ -13,7 +13,7 @@
 
 CHUNKS = 4
 PIECES = 16
-UNITS = 2
+UNITS = 1
 
 TEXT_ROUTE = (24, 16, 8, 1, 24, 16, 8, 6, 24, 16, 8, 14, 17, 9, 1, 6)
 LATE_ORDER = (0, 1, -1, -2, -3, 2, 3, -4)

time: 49.7 us -> 49.3 us (level)
  no operation moved by 1% of the time
where the time goes in v4:
time: 49.3 us; the launch traced here: 49.1 us
  Pallas kernels  44.6 us (90%)
  local copies, waits for them, and re-layouts  2.59 us (5%)
  between operations  1.93 us (4%)
    pallas_call x1, Pallas kernels, per_device(): pl.pallas_call(kernel, out_shape=(grad, grad, jax.ShapeDtypeStruct((1, ro...  44.6 us
    unnamed x3, local copies, waits for them, and re-layouts  2.59 us

profile of v4, /device:TPU:255, one launch (start us, length us, event | category | flops | bytes accessed | tf_op | source)
XLA Modules:
  0.0 49.1 jit_solution(13706892888007922340)
XLA Ops:
  1.9 44.6 %shard_map.67 = (f32[256,1152]{1,0:T(8,128)S(1)}, f32[256,1152]{1,0:T(8,128)S(1)}, f32[1,256]{1,0:T(1,128)S(1)}) custom-call(f32[1]{0:T(128)S(6)} %copy.10.scale_ref, f32[1]{0:T(128)S(6)} %copy.11.bias_ref, f32[256,1152]{1,0:T(8,128)} %image_hbm.1, f32[256,1152]{1,0:T(8,128)} %text_hbm.1), custom_call_target="tpu_custom_call" | custom-call | tf_op jit(solution)/shard_map/pallas_call | solution.py:430
  46.5 1.0 %copy.12 = f32[256,1152]{1,0:T(8,128)} copy(f32[256,1152]{1,0:T(8,128)S(1)} %get-tuple-element.12) | data formatting | bytes 2359296
  47.5 1.0 %copy.13 = f32[256,1152]{1,0:T(8,128)} copy(f32[256,1152]{1,0:T(8,128)S(1)} %get-tuple-element.13) | data formatting | bytes 2359296
  48.5 0.6 %copy.14 = f32[256]{0:T(256)} copy(f32[256]{0:T(256)S(1)} %bitcast.1) | data formatting | bytes 2048
